TPU v7x, 32 devices: a whole 2x2x4 slice. The times are simulated.
32 devices in a mesh: req: 4 (over y, x), exp: 8 (over z, core).
Axes of the slice: x: 2, y: 2, z: 4, core: 2. Of those that a mesh axis runs over, the one named last changes fastest.
Arguments:
- hidden: bfloat16 [8, 512, 2048], P('req', 'exp'), may hold values from -6 to 6
- q_new: bfloat16 [8, 16, 512, 128], P('req', None, 'exp'), may hold values from -480 to 480
- k_new: bfloat16 [8, 16, 512, 128], P('req', None, 'exp'), may hold values from -6 to 6
- v_new: bfloat16 [8, 16, 512, 128], P('req', None, 'exp'), may hold values from -6 to 6
- routes: int32 [8, 512, 6], P('req', 'exp'), may hold values from 0 to 63, all different within a row; in each aligned block of 64 rows (0 to 63, 64 to 127, ..., all dimensions but the last counted through in order) at most 8 rows name the same one
- slot_request: int32 [8], replicated, may hold values from 0 to 7, each once
- lengths: int32 [8], replicated, may hold values from 5 to 16384, as said below
- cycle_cache: bfloat16 [128, 2, 4096, 128], P(('req', 'exp')), may hold values from -6 to 6
- sink_cache: bfloat16 [128, 2, 4, 128], P(('req', 'exp')), may hold values from -6 to 6
- w_out: bfloat16 [2048, 2048], replicated, may hold values from -0.125 to 0.125
- norm_gain: float32 [2048], replicated, may hold values from 0.5 to 1.5
- router: bfloat16 [2048, 64], replicated, may hold values from -0.125 to 0.125
- w_gate: bfloat16 [2048, 90112], P(None, ('req', 'exp')), may hold values from -0.125 to 0.125
- w_up: bfloat16 [2048, 90112], P(None, ('req', 'exp')), may hold values from -0.125 to 0.125
- w_down: bfloat16 [90112, 2048], P(('req', 'exp')), may hold values from -0.15625 to 0.15625
Outputs:
- layer_out: bfloat16 [8, 512, 2048], P('req', 'exp')
- cycle_out: bfloat16 [128, 2, 4096, 128], P(('req', 'exp'))
Inputs may be any that keep to these rules, and one draw needn't show every extreme that they name: In every aligned block of 64 rows of routes (the rows of one request on one index of exp) no expert is named by more than 8 rows, a bound that some block reaches. `slot_request`: each request once. `lengths`: some slot has exactly 16384 cached tokens, and some other fewer than 2048.
All inputs are finite; a program needn't handle non-finite values.
Results may differ from a plain program's by a relative error of at most 0.014.
The roundings to bfloat16 on the way count: a program that leaves them out, or rounds other values in their place, can miss the bound.
Values may be sent and summed in bfloat16 or wider, within the bound.
A program may use at most 192 MiB of HBM per device.

v0:
```python
import functools

import jax
import jax.numpy as jnp
from jax import lax
from jax.experimental import pallas as pl
from jax.experimental.pallas import tpu as pltpu
from jax.sharding import PartitionSpec as P

SPLIT = 2
SINK_PAD = 128
ALIGN = 32
LOG2E = 1.4426950408889634


def angle_tables(length, seq_len, head_dim):
    half_width = head_dim // 2
    positions = length + jnp.arange(seq_len, dtype=jnp.int32)
    frequency = 10000.0 ** (-2.0 * jnp.arange(half_width, dtype=jnp.float32) / head_dim)
    angles = positions.astype(jnp.float32)[:, None] * frequency[None, :]
    cosine = jnp.cos(angles)
    sine = jnp.sin(angles)
    return (
        jnp.concatenate([cosine, cosine], axis=-1),
        jnp.concatenate([-sine, sine], axis=-1),
    )


def attend_kernel(
    sinks,
    tile_keys,
    tile_rows,
    length_ref,
    fresh_ref,
    cycle_ref,
    sink_ref,
    cosine_ref,
    sine_ref,
    context_ref,
    updated_ref,
    query,
    extra_key,
    extra_value,
    stage,
    blend,
    highest,
):
    seq_len, head_dim = query.shape
    window = cycle_ref.shape[2]
    length = length_ref[0]
    offset = lax.rem(length, window)
    factor = head_dim ** (-0.5) * LOG2E

    def turned(index):
        rows = fresh_ref[:, index, 0].reshape(seq_len, head_dim).astype(jnp.float32)
        return rows * cosine_ref[...] + pltpu.roll(rows, head_dim // 2, 1) * sine_ref[...]

    query[...] = turned(0).astype(jnp.bfloat16)
    key_turned = turned(1)
    value_rows = fresh_ref[:, 2, 0].reshape(seq_len, head_dim)
    stage[0, ALIGN : ALIGN + seq_len] = key_turned
    stage[1, ALIGN : ALIGN + seq_len] = value_rows.astype(jnp.float32)
    extra_key[:seq_len] = key_turned.astype(jnp.bfloat16)
    extra_value[:seq_len] = value_rows
    extra_key[seq_len:] = sink_ref[0, 0]
    extra_value[seq_len:] = sink_ref[0, 1]

    def blended(weights, values):
        wide = jnp.concatenate([values, jnp.ones_like(values)], axis=1)
        return jnp.dot(weights.astype(jnp.bfloat16), wide, preferred_element_type=jnp.float32)

    def dots(rows, keys):
        return lax.dot_general(
            rows, keys, (((1,), (1,)), ((), ())), preferred_element_type=jnp.float32
        )

    def first(block, carry):
        start = pl.multiple_of(block * tile_rows, tile_rows)
        here = pl.ds(start, tile_rows)
        scores = dots(query[here, :], extra_key[...])
        width = seq_len + SINK_PAD
        row = start + lax.broadcasted_iota(jnp.int32, (tile_rows, 1), 0)
        column = lax.broadcasted_iota(jnp.int32, (1, width), 1)
        sink_limit = jnp.minimum(length + row - window, sinks - 1) + seq_len
        is_new = column < seq_len
        new_key = jnp.where(is_new, column, window)
        sink_key = jnp.where(is_new, 2 * window + seq_len, column)
        seen = (new_key <= row) | (sink_key <= sink_limit)
        scores = jnp.where(seen, scores, -jnp.inf)
        top = jnp.max(scores, axis=1, keepdims=True)
        weights = jnp.exp2((scores - top) * factor)
        blend[here, :] = blended(weights, extra_value[...])
        highest[here, :] = jnp.broadcast_to(top, (tile_rows, head_dim))
        return carry

    lax.fori_loop(0, seq_len // tile_rows, first, 0)

    def tile(number, carry):
        slot_start = pl.multiple_of(number * tile_keys, tile_keys)
        keys_here = pl.ds(slot_start, tile_keys)
        age_start = lax.rem(slot_start - offset + window, window)
        partial = (age_start < seq_len) | (age_start + tile_keys > window) | (length < window)

        def rows_step(masked, start):
            here = pl.ds(start, tile_rows)
            scores = dots(query[here, :], cycle_ref[0, 0, keys_here, :])
            if masked:
                row = start + lax.broadcasted_iota(jnp.int32, (tile_rows, 1), 0)
                column = lax.broadcasted_iota(jnp.int32, (1, tile_keys), 1)
                age = column + age_start
                age = jnp.where(age >= window, age - window, age)
                scores = jnp.where(age >= jnp.maximum(row + 1, window - length), scores, -jnp.inf)
            before = highest[here, :]
            top = jnp.maximum(before[:, :1], jnp.max(scores, axis=1, keepdims=True))
            weights = jnp.exp2((scores - top) * factor)
            keep = jnp.exp2((before[:, :1] - top) * factor)
            blend[here, :] = blend[here, :] * keep + blended(
                weights, cycle_ref[0, 1, keys_here, :]
            )
            highest[here, :] = jnp.broadcast_to(top, (tile_rows, head_dim))

        def all_rows(masked):
            pairs = 2 if (seq_len // tile_rows) % 2 == 0 else 1

            def body(step, inner):
                for part in range(pairs):
                    start = pl.multiple_of((step * pairs + part) * tile_rows, tile_rows)
                    rows_step(masked, start)
                return inner

            lax.fori_loop(0, seq_len // tile_rows // pairs, body, 0)

        live = slot_start < length

        @pl.when(live & partial)
        def _():
            all_rows(True)

        @pl.when(live & jnp.logical_not(partial))
        def _():
            all_rows(False)

        return carry

    lax.fori_loop(0, window // tile_keys, tile, 0)

    total = blend[:, head_dim:]
    context = (blend[:, :head_dim] / total).astype(jnp.bfloat16)
    context_ref[:, 0] = context.reshape(context_ref.shape[0], context_ref.shape[2], head_dim)

    updated_ref[...] = cycle_ref[...]
    base = lax.div(offset, ALIGN) * ALIGN
    shift = offset - base

    def put(chunk, carry):
        at = pl.multiple_of(lax.rem(base + chunk * ALIGN, window), ALIGN)
        fresh_row = (
            chunk * ALIGN - shift + lax.broadcasted_iota(jnp.int32, (ALIGN, head_dim), 0)
        )
        inside = (fresh_row >= 0) & (fresh_row < seq_len)
        for which in range(2):
            fresh = stage[which, pl.ds(ALIGN + chunk * ALIGN - shift, ALIGN), :]
            old = updated_ref[0, which, pl.ds(at, ALIGN), :].astype(jnp.float32)
            updated_ref[0, which, pl.ds(at, ALIGN), :] = jnp.where(inside, fresh, old).astype(
                jnp.bfloat16
            )
        return carry

    lax.fori_loop(0, seq_len // ALIGN + 1, put, 0)


def attend(fresh, cycle_cache, sink_cache, length):
    members, _, pairs, local_rows, head_dim = fresh.shape
    seq_len = members * local_rows
    window = cycle_cache.shape[2]
    sinks = sink_cache.shape[2]
    tile_keys = min(1024, window)
    tile_rows = min(256, seq_len)
    cosine, sine = angle_tables(length, seq_len, head_dim)
    sink_wide = jnp.pad(sink_cache, ((0, 0), (0, 0), (0, SINK_PAD - sinks), (0, 0)))
    return pl.pallas_call(
        functools.partial(attend_kernel, sinks, tile_keys, tile_rows),
        out_shape=(
            jax.ShapeDtypeStruct((members, pairs, local_rows, head_dim), jnp.bfloat16),
            jax.ShapeDtypeStruct(cycle_cache.shape, cycle_cache.dtype),
        ),
        grid_spec=pltpu.PrefetchScalarGridSpec(
            num_scalar_prefetch=1,
            grid=(pairs,),
            in_specs=[
                pl.BlockSpec((members, 3, 1, local_rows, head_dim), lambda p, _: (0, 0, p, 0, 0)),
                pl.BlockSpec((1, 2, window, head_dim), lambda p, _: (p, 0, 0, 0)),
                pl.BlockSpec((1, 2, SINK_PAD, head_dim), lambda p, _: (p, 0, 0, 0)),
                pl.BlockSpec((seq_len, head_dim), lambda p, _: (0, 0)),
                pl.BlockSpec((seq_len, head_dim), lambda p, _: (0, 0)),
            ],
            out_specs=[
                pl.BlockSpec((members, 1, local_rows, head_dim), lambda p, _: (0, p, 0, 0)),
                pl.BlockSpec((1, 2, window, head_dim), lambda p, _: (p, 0, 0, 0)),
            ],
            scratch_shapes=[
                pltpu.VMEM((seq_len, head_dim), jnp.bfloat16),
                pltpu.VMEM((seq_len + SINK_PAD, head_dim), jnp.bfloat16),
                pltpu.VMEM((seq_len + SINK_PAD, head_dim), jnp.bfloat16),
                pltpu.VMEM((2, seq_len + 2 * ALIGN, head_dim), jnp.float32),
                pltpu.VMEM((seq_len, 2 * head_dim), jnp.float32),
                pltpu.VMEM((seq_len, head_dim), jnp.float32),
            ],
        ),
        compiler_params=pltpu.CompilerParams(vmem_limit_bytes=48 * 1024 * 1024),
        cost_estimate=pl.CostEstimate(
            flops=4 * pairs * seq_len * (window + seq_len) * head_dim,
            bytes_accessed=4 * cycle_cache.size,
            transcendentals=pairs * seq_len * (window + seq_len),
        ),
    )(length.reshape(1), fresh, cycle_cache, sink_wide, cosine, sine)


def on_device(
    hidden,
    q_new,
    k_new,
    v_new,
    routes,
    slot_request,
    lengths,
    cycle_cache,
    sink_cache,
    w_out,
    norm_gain,
    router,
    w_gate,
    w_up,
    w_down,
):
    group_width = lax.axis_size("exp")
    group_count = lax.axis_size("req")
    devices_all = group_count * group_width
    group_index = lax.axis_index("req")
    member_index = lax.axis_index("exp")
    slots_here, local_rows, model_width = hidden.shape
    head_count = q_new.shape[1]
    head_dim = q_new.shape[3]
    experts_all = router.shape[1]
    pair_count = slots_here * head_count
    pairs_here = pair_count // group_width
    members_of_slot = head_count // pairs_here

    requests = lax.dynamic_slice_in_dim(slot_request, group_index * slots_here, slots_here)
    fresh_all = lax.all_gather(jnp.stack([q_new, k_new, v_new], 1), "req", axis=0, tiled=True)
    fresh_sel = jnp.take(fresh_all, requests, axis=0)
    fresh_out = (
        fresh_sel.reshape(
            slots_here, 3, members_of_slot, pairs_here, local_rows, head_dim
        )
        .transpose(0, 2, 1, 3, 4, 5)
        .reshape(group_width, 3, pairs_here, local_rows, head_dim)
    )
    fresh = lax.all_to_all(fresh_out, "exp", split_axis=0, concat_axis=0, tiled=True)
    slot_here = group_index * slots_here + member_index // members_of_slot
    length = lax.dynamic_index_in_dim(lengths, slot_here, keepdims=False)

    hidden_sel = jnp.take(lax.all_gather(hidden, "req", axis=0, tiled=True), requests, axis=0)
    route_sel = jnp.take(lax.all_gather(routes, "req", axis=0, tiled=True), requests, axis=0)
    route_group = lax.all_gather(route_sel, "exp", axis=0)

    context, cycle_out = attend(fresh, cycle_cache, sink_cache, length)
    context_rows = lax.all_to_all(context, "exp", split_axis=0, concat_axis=0, tiled=True)
    context_rows = context_rows.reshape(slots_here, head_count, local_rows, head_dim)
    projected = jnp.einsum(
        "shqd,hde->sqe",
        context_rows,
        w_out.reshape(head_count, head_dim, model_width),
        preferred_element_type=jnp.float32,
    )
    residual = hidden_sel.astype(jnp.float32) + projected
    inverse = lax.rsqrt(jnp.mean(residual * residual, axis=-1, keepdims=True) + 1e-06)
    normed = (residual * inverse * norm_gain).astype(jnp.bfloat16)

    blocks = group_width * slots_here
    most_slots = max(2, local_rows // 8)
    sub_here = experts_all * SPLIT // devices_all
    units = max(1, sub_here // SPLIT)
    pieces = max(1, SPLIT // sub_here)
    owners = jnp.arange(group_count, dtype=jnp.int32) * group_width + member_index
    served = (
        owners[:, None] * units + jnp.arange(units, dtype=jnp.int32)[None, :]
    ).reshape(-1) // pieces
    served_count = group_count * units
    route_blocks = route_group.reshape(blocks, local_rows, -1)
    named = jnp.any(route_blocks[..., None] == served, axis=2)
    earlier_rows = jnp.arange(local_rows)[:, None] > jnp.arange(local_rows)[None, :]
    earlier = jnp.einsum(
        "qp,bpe->bqe",
        earlier_rows.astype(jnp.bfloat16),
        named.astype(jnp.bfloat16),
        preferred_element_type=jnp.float32,
    ).astype(jnp.int32)
    chosen = named[..., None] & (
        earlier[..., None] == jnp.arange(most_slots, dtype=jnp.int32)
    )

    rows_group = lax.all_gather(normed, "exp", axis=0).reshape(blocks, local_rows, model_width)
    outgoing = jnp.einsum(
        "bqer,bqd->ebrd",
        chosen.astype(jnp.bfloat16),
        rows_group,
        preferred_element_type=jnp.float32,
    ).astype(jnp.bfloat16)
    landed = lax.all_to_all(
        outgoing.reshape(group_count, units, blocks * most_slots, model_width),
        "req",
        split_axis=0,
        concat_axis=0,
        tiled=True,
    )
    logits = jnp.einsum("bqd,de->bqe", rows_group, router, preferred_element_type=jnp.float32)
    routed = jnp.any(
        route_blocks[..., None] == jnp.arange(experts_all, dtype=jnp.int32), axis=2
    )
    logits = jnp.where(routed, logits, -jnp.inf)
    gates_all = jax.nn.softmax(logits, axis=-1)
    gates = jnp.take(gates_all, served, axis=2)
    weights = jnp.where(chosen, gates[..., None], 0.0)
    weights_high = lax.reduce_precision(weights, 8, 7)
    weights_low = (weights - weights_high).astype(jnp.bfloat16)
    weights_high = weights_high.astype(jnp.bfloat16)

    hidden_units = w_gate.shape[1] // units
    replies = []
    for unit in range(units):
        rows = landed[:, unit].reshape(group_count * blocks * most_slots, model_width)
        span = slice(unit * hidden_units, (unit + 1) * hidden_units)
        gate_part = jnp.dot(rows, w_gate[:, span], preferred_element_type=jnp.float32)
        up_part = jnp.dot(rows, w_up[:, span], preferred_element_type=jnp.float32)
        active = (jax.nn.silu(gate_part) * up_part).astype(jnp.bfloat16)
        reply = jnp.dot(active, w_down[span], preferred_element_type=jnp.float32)
        replies.append(
            reply.astype(jnp.bfloat16).reshape(
                group_count, 1, blocks * most_slots, model_width
            )
        )
    reply = replies[0] if units == 1 else jnp.concatenate(replies, 1)
    returned = lax.all_to_all(reply, "req", split_axis=0, concat_axis=0, tiled=True).reshape(
        served_count, blocks, most_slots, model_width
    )

    def combined(part):
        return jnp.einsum("bqer,ebrd->bqd", part, returned, preferred_element_type=jnp.float32)

    partial = (combined(weights_high) + combined(weights_low)).astype(jnp.bfloat16)
    moe = lax.psum_scatter(
        partial.reshape(group_width, slots_here, local_rows, model_width),
        "exp",
        scatter_dimension=0,
        tiled=False,
    )
    layer_out = (residual + moe.astype(jnp.float32)).astype(jnp.bfloat16)
    return (layer_out, cycle_out)


def solution(mesh):
    in_specs = (
        P("req", "exp", None),
        P("req", None, "exp", None),
        P("req", None, "exp", None),
        P("req", None, "exp", None),
        P("req", "exp", None),
        P(),
        P(),
        P(("req", "exp"), None, None, None),
        P(("req", "exp"), None, None, None),
        P(),
        P(),
        P(),
        P(None, ("req", "exp")),
        P(None, ("req", "exp")),
        P(("req", "exp"), None),
    )
    out_specs = (P("req", "exp", None), P(("req", "exp"), None, None, None))
    return jax.shard_map(
        on_device, mesh=mesh, in_specs=in_specs, out_specs=out_specs, check_vma=False
    )
```

profile of v0, /device:TPU:0, one launch (start us, length us, event | category | flops | bytes accessed | tf_op | source)
XLA Modules:
  0.0 453.0 jit_solution(5367703743853276448)
XLA Ops:
  7.2 2.7 pad_maximum_fusion.1
  10.0 73.3 %all-gather.7.cloned.1.call-done = bf16[8,3,16,64,128]{4,3,2,0,1:T(8,128)(2,1)} async-done(((bf16[2,3,16,64,128]{4,3,2,0,1:T(8,128)(2,1)}), bf16[8,3,16,64,128]{4,3,2,0,1:T(8,128)(2,1)}) %all-gather.7.cloned.1.call-update) | async-done | bytes 6291472 | tf_op jit(solution)/shard_map/all_gather | solution.py:250
  83.3 3.6 gather_fusion.1
  87.0 0.2 broadcast_select_fusion
  87.2 0.1 fusion.73
  87.3 1.3 pad_maximum_fusion.2
  88.7 4.6 %all-to-all-start = ((bf16[8,3,4,64,128]{4,3,2,1,0:T(8,128)(2,1)}), bf16[8,3,4,64,128]{4,3,2,1,0:T(8,128)(2,1)S(1)}, u32[]{:S(2)}, u32[]{:S(2)}) async-start(bf16[8,3,4,64,128]{4,3,2,1,0:T(8,128)(2,1)} %bitcast.3), calls=%async_computation | async-start | bytes 3145728 | tf_op jit(solution)/shard_map/all_to_all | solution.py:259
  93.3 0.7 all-gather.5.cloned.1.call-update
  94.1 0.6 dynamic_slice.8.length_ref
  94.8 0.6 add_convert_fusion
  95.4 1.0 fusion.63
  96.4 0.2 pad_maximum_fusion.3
  96.6 34.5 %all-to-all-done.fresh_ref = bf16[8,3,4,64,128]{4,3,2,1,0:T(8,128)(2,1)S(1)} async-done(((bf16[8,3,4,64,128]{4,3,2,1,0:T(8,128)(2,1)}), bf16[8,3,4,64,128]{4,3,2,1,0:T(8,128)(2,1)S(1)}, u32[]{:S(2)}, u32[]{:S(2)}) %all-to-all-start) | async-done | bytes 1572896 | tf_op jit(solution)/shard_map/all_to_all | solution.py:259
  131.1 33.1 %shard_map.158 = (bf16[8,4,64,128]{3,2,1,0:T(8,128)(2,1)}, bf16[4,2,4096,128]{3,2,1,0:T(8,128)(2,1)}) custom-call(s32[1]{0:T(128)} %dynamic_slice.8.length_ref, bf16[8,3,4,64,128]{4,3,2,1,0:T(8,128)(2,1)S(1)} %all-to-all-done.fresh_ref, bf16[4,2,4096,128]{3,2,1,0:T(8,128)(2,1)} %cycle_ref.1, bf16[4,2,128,128]{3,2,1,0:T(8,128)(2,1)S(1)} %pad.4.sink_ref, ...), custom_call_target="tpu_custom_call" | custom-call | flops 4831838208 | bytes 16777216 | tf_op jit(solution)/shard_map/pallas_call | solution.py:181
  164.2 3.5 all-to-all-start.1
  167.8 2.2 gather_fusion
  170.0 13.0 %all-to-all-done.1 = bf16[8,4,64,128]{3,2,1,0:T(8,128)(2,1)S(1)} async-done(((bf16[8,4,64,128]{3,2,1,0:T(8,128)(2,1)}), bf16[8,4,64,128]{3,2,1,0:T(8,128)(2,1)S(1)}, u32[]{:S(2)}, u32[]{:S(2)}) %all-to-all-start.1) | async-done | bytes 524320 | tf_op jit(solution)/shard_map/all_to_all | solution.py:268
  183.0 4.9 %multiply_reduce_fusion = (f32[2,64]{1,0:T(2,128)S(1)}, f32[2,64,2048]{2,1,0:T(8,128)S(1)}) fusion(bf16[16,128,2048,1]{2,1,0,3:T(8,128)(2,1)} %bitcast.77, bf16[2,64,2048]{2,1,0:T(8,128)(2,1)S(1)} %gather_fusion, pred[2]{0:T(512)(128)(4,1)S(1)} %get-tuple-element.6, bf16[2,16,64,128]{3,2,1,0:T(8,128)(2,1)S(1)} %bitcast.78), kind=kOutput, calls=%fused_computation.46 | convolution fusion | flops 1075052416 | bytes 10486274 | tf_op jit(solution)/shard_map/shqd,hde->sqe/dot_general | solution.py:270
  187.9 1.0 multiply_convert_fusion
  188.9 0.6 copy-done.2
  189.6 8.7 %all_gather.21 = s32[8,64,6]{1,2,0:T(8,128)S(1)} all-gather(s32[2,64,6]{1,2,0:T(8,128)S(1)} %copy.46), channel_id=1, replica_groups=mesh['req'=4,'exp'=8] {'req'}, dimensions={0}, use_global_device_ids=true | all-gather | bytes 15360 | tf_op jit(solution)/shard_map/all_gather | solution.py:264
  198.3 0.5 gather_fusion.2
  198.9 14.2 %all_gather.22 = s32[8,2,64,6]{2,1,3,0:T(2,128)S(1)} all-gather(s32[1,2,64,6]{2,1,3,0:T(2,128)S(1)} %copy.47), channel_id=1, replica_groups=mesh['req'=4,'exp'=8] {'exp'}, dimensions={0}, use_global_device_ids=true | all-gather | bytes 27648 | tf_op jit(solution)/shard_map/all_gather | solution.py:265
  213.2 0.1 compare_reduce_fusion
  213.3 0.1 fusion.44
  213.5 21.5 %all-gather.9.cloned.1.call-done = bf16[16,64,2048]{2,1,0:T(8,128)(2,1)} async-done(((bf16[2,64,2048]{2,1,0:T(8,128)(2,1)}), bf16[16,64,2048]{2,1,0:T(8,128)(2,1)}) %all-gather.9.cloned.1.call-update) | async-done | bytes 4194320 | tf_op jit(solution)/shard_map/all_gather | solution.py:303
  235.0 3.4 fusion.23
  238.5 0.3 copy.56
  238.8 51.9 %all_to_all.20 = bf16[4,2,128,2048]{3,2,1,0:T(8,128)(2,1)S(1)} all-to-all(bf16[4,2,128,2048]{3,2,1,0:T(8,128)(2,1)S(1)} %bitcast.76), channel_id=1, replica_groups=mesh['req'=4,'exp'=8] {'req'}, dimensions={0} | all-to-all | bytes 8388608 | tf_op jit(solution)/shard_map/all_to_all | solution.py:310
  290.7 0.4 fusion.72
  291.2 2.5 slice-done.2
  293.7 5.1 %fusion.6 = f32[512,1408]{1,0:T(8,128)} fusion(bf16[512,2048]{1,0:T(8,128)(2,1)S(1)} %bitcast.81, bf16[2048,2816]{1,0:T(8,128)(2,1)S(1)} %bitcast.90), kind=kOutput, calls=%fused_computation.12 | convolution fusion | flops 2952790016 | bytes 10747904 | tf_op jit(solution)/shard_map/dot_general | solution.py:334
  298.8 5.1 %fusion.12 = f32[512,1408]{1,0:T(8,128)} fusion(bf16[512,2048]{1,0:T(8,128)(2,1)S(1)} %bitcast.79, bf16[2048,2816]{1,0:T(8,128)(2,1)S(1)} %bitcast.90), kind=kOutput, calls=%fused_computation.18 | convolution fusion | flops 2952790016 | bytes 10747904 | tf_op jit(solution)/shard_map/dot_general | solution.py:334
  303.8 13.8 %fusion.34 = bf16[512,2048]{1,0:T(8,128)(2,1)} fusion(bf16[2816,2048]{1,0:T(8,128)(2,1)} %param.29, bf16[512,2048]{1,0:T(8,128)(2,1)} %bitcast.82, bf16[2048,2816]{1,0:T(8,128)(2,1)} %param.28, f32[512,1408]{1,0:T(8,128)} %fusion.6), kind=kOutput, calls=%fused_computation.32 | convolution fusion | flops 5910953984 | bytes 18612224 | tf_op jit(solution)/shard_map/dot_general | solution.py:337
  317.6 13.5 %fusion.31 = bf16[512,2048]{1,0:T(8,128)(2,1)} fusion(bf16[2816,2048]{1,0:T(8,128)(2,1)} %param.29, bf16[512,2048]{1,0:T(8,128)(2,1)S(1)} %bitcast.80, bf16[2048,2816]{1,0:T(8,128)(2,1)} %param.28, f32[512,1408]{1,0:T(8,128)} %fusion.12), kind=kOutput, calls=%fused_computation.31 | convolution fusion | flops 5910953984 | bytes 18612224 | tf_op jit(solution)/shard_map/dot_general | solution.py:337
  331.0 4.6 %pad_maximum_fusion = bf16[4,2,128,2048]{3,2,1,0:T(8,128)(2,1)} fusion(bf16[4,1,128,2048]{3,2,1,0:T(8,128)(2,1)} %bitcast.83, bf16[4,1,128,2048]{3,2,1,0:T(8,128)(2,1)} %bitcast.84), kind=kLoop, calls=%fused_computation.20 | loop fusion | flops 2097152 | bytes 8388608 | tf_op jit(solution)/shard_map/concatenate | solution.py:343
  335.7 5.1 %all-to-all-start.3 = ((bf16[4,2,128,2048]{3,2,1,0:T(8,128)(2,1)}), bf16[4,2,128,2048]{3,2,1,0:T(8,128)(2,1)}, u32[]{:S(2)}, u32[]{:S(2)}) async-start(bf16[4,2,128,2048]{3,2,1,0:T(8,128)(2,1)} %pad_maximum_fusion), calls=%async_computation.3 | async-start | bytes 8388608 | tf_op jit(solution)/shard_map/all_to_all | solution.py:344
  340.8 0.1 add.139
  340.9 1.2 fusion.24
  342.1 0.2 copy.53
  342.3 4.3 fusion.74
  346.8 0.3 copy.54
  347.1 0.6 gather_fusion.3
  347.7 39.6 %all-to-all-done.3 = bf16[4,2,128,2048]{3,2,1,0:T(8,128)(2,1)} async-done(((bf16[4,2,128,2048]{3,2,1,0:T(8,128)(2,1)}), bf16[4,2,128,2048]{3,2,1,0:T(8,128)(2,1)}, u32[]{:S(2)}, u32[]{:S(2)}) %all-to-all-start.3) | async-done | bytes 4194336 | tf_op jit(solution)/shard_map/all_to_all | solution.py:344
  387.3 3.5 fusion.15
  390.8 5.6 %fusion.1 = bf16[16,64,2048]{2,1,0:T(8,128)(2,1)} fusion(f32[16,64,2048,1]{2,1,3,0:T(8,128)S(1)} %fusion.15, bf16[8,16,8,2048]{3,2,1,0:T(8,128)(2,1)} %bitcast.27, f32[16,64,8]{1,2,0:T(8,128)S(1)} %copy.55, s32[16,64,8]{1,2,0:T(8,128)S(1)} %copy.51, pred[16,64,8]{1,2,0:T(8,128)(4,1)S(1)} %compare_reduce_fusion), kind=kOutput, calls=%fused_computation.6 | convolution fusion | flops 273022976 | bytes 16850944 | tf_op jit(solution)/shard_map/bqer,ebrd->bqd/dot_general | solution.py:349
  396.5 48.0 %reduce-scatter.2.cloned.1.call-done = bf16[1,2,64,2048]{3,2,1,0:T(8,128)(2,1)} async-done(((bf16[8,2,64,2048]{3,2,1,0:T(8,128)(2,1)}), bf16[1,2,64,2048]{3,2,1,0:T(8,128)(2,1)}) %reduce-scatter.2.cloned.1.call-update) | async-done | bytes 524304 | tf_op jit(solution)/shard_map/reduce_scatter | solution.py:352
  444.5 1.9 fusion.45
  (55 shorter events, 0.9 us)
Async XLA Ops:
  7.2 335.2 %copy-start = (bf16[2048,64]{0,1:T(8,128)(2,1)S(1)}, bf16[2048,64]{0,1:T(8,128)(2,1)}, u32[]{:S(2)}) copy-start(bf16[2048,64]{0,1:T(8,128)(2,1)} %param.26) | copy-start | bytes 786436
  7.2 2.8 copy-start.9
  7.2 76.1 %all-gather.7.cloned.1.call-start = ((), (), s32[]{:S(2)}) async-start(), calls=%async_computation.6 | async-start | bytes 7864320 | tf_op jit(solution)/shard_map/all_gather | solution.py:250
  87.3 6.7 %copy-start.10 = (s32[8]{0:T(128)S(1)}, s32[8]{0:T(128)}, u32[]{:S(2)}) copy-start(s32[8]{0:T(128)} %param.21) | copy-start | bytes 100
  87.3 7.4 %copy-start.5 = (bf16[4,2,4,128]{3,2,1,0:T(4,128)(2,1)S(1)}, bf16[4,2,4,128]{3,2,1,0:T(4,128)(2,1)}, u32[]{:S(2)}) copy-start(bf16[4,2,4,128]{3,2,1,0:T(4,128)(2,1)} %param.23) | copy-start | bytes 24580
  88.7 42.4 %all-to-all-start = ((bf16[8,3,4,64,128]{4,3,2,1,0:T(8,128)(2,1)}), bf16[8,3,4,64,128]{4,3,2,1,0:T(8,128)(2,1)S(1)}, u32[]{:S(2)}, u32[]{:S(2)}) async-start(bf16[8,3,4,64,128]{4,3,2,1,0:T(8,128)(2,1)} %bitcast.3), calls=%async_computation | async-start | bytes 3145728 | tf_op jit(solution)/shard_map/all_to_all | solution.py:259
  93.3 74.5 %all-gather.5.cloned.1.call-start = ((), (), s32[]{:S(2)}) async-start(), calls=%async_computation.5 | async-start | bytes 2621440 | tf_op jit(solution)/shard_map/all_gather | solution.py:263
  164.2 18.8 %all-to-all-start.1 = ((bf16[8,4,64,128]{3,2,1,0:T(8,128)(2,1)}), bf16[8,4,64,128]{3,2,1,0:T(8,128)(2,1)S(1)}, u32[]{:S(2)}, u32[]{:S(2)}) async-start(bf16[8,4,64,128]{3,2,1,0:T(8,128)(2,1)} %get-tuple-element.4), calls=%async_computation.1 | async-start | bytes 1048576 | tf_op jit(solution)/shard_map/all_to_all | solution.py:268
  167.7 67.3 %all-gather.9.cloned.1.call-start = ((), (), s32[]{:S(2)}) async-start(), calls=%async_computation.8 | async-start | bytes 4718592 | tf_op jit(solution)/shard_map/all_gather | solution.py:303
  183.0 4.9 %copy-start.4 = (f32[2048]{0:T(1024)S(1)}, f32[2048]{0:T(1024)}, u32[]{:S(2)}) copy-start(f32[2048]{0:T(1024)} %param.25) | copy-start | bytes 24580
  183.0 6.6 %copy-start.6 = (s32[2,64,6]{1,0,2:T(2,128)S(1)}, s32[2,64,6]{1,0,2:T(2,128)}, u32[]{:S(2)}) copy-start(s32[2,64,6]{1,0,2:T(2,128)} %param.19) | copy-start | bytes 9220
  188.9 0.6 copy-start.2
  189.6 48.9 %copy-start.7 = (s32[8]{0:T(128)}, s32[8]{0:T(128)S(1)}, u32[]{:S(2)}) copy-start(s32[8]{0:T(128)S(1)} %add.135) | copy-start | bytes 100
  238.5 52.7 %slice-start = ((s8[11534336]{0:T(1024)(128)(4,1)}), s8[3145728]{0:T(1024)(128)(4,1)S(1)}, s32[]{:S(2)}) async-start(s8[11534336]{0:T(1024)(128)(4,1)} %bitcast.89), calls=%async_computation.9 | async-start | bytes 6291456
  238.8 52.4 %slice-start.1 = ((s8[11534336]{0:T(1024)(128)(4,1)}), s8[4194304]{0:T(1024)(128)(4,1)S(1)}, s32[]{:S(2)}) async-start(s8[11534336]{0:T(1024)(128)(4,1)} %bitcast.89), calls=%async_computation.10 | async-start | bytes 8388608
  290.7 2.9 slice-start.2
  291.2 7.6 %copy-start.1 = (bf16[4,1,128,2048]{3,2,1,0:T(8,128)(2,1)}, bf16[4,1,128,2048]{3,2,1,0:T(8,128)(2,1)S(1)}, u32[]{:S(2)}) copy-start(bf16[4,1,128,2048]{3,2,1,0:T(8,128)(2,1)S(1)} %get-tuple-element.9) | copy-start | bytes 6291460
  335.7 5.1 %copy-start.3 = (s32[4,2]{1,0:T(4,128)S(1)}, s32[4,2]{1,0:T(4,128)}, u32[]{:S(2)}) copy-start(s32[4,2]{1,0:T(4,128)} %copy-done.2) | copy-start | bytes 100
  335.7 6.7 %copy-start.8 = (s32[8]{0:T(128)S(1)}, s32[8]{0:T(128)}, u32[]{:S(2)}) copy-start(s32[8]{0:T(128)} %copy-done.7) | copy-start | bytes 100
  335.7 51.7 %all-to-all-start.3 = ((bf16[4,2,128,2048]{3,2,1,0:T(8,128)(2,1)}), bf16[4,2,128,2048]{3,2,1,0:T(8,128)(2,1)}, u32[]{:S(2)}, u32[]{:S(2)}) async-start(bf16[4,2,128,2048]{3,2,1,0:T(8,128)(2,1)} %pad_maximum_fusion), calls=%async_computation.3 | async-start | bytes 8388608 | tf_op jit(solution)/shard_map/all_to_all | solution.py:344
  340.7 103.8 %reduce-scatter.2.cloned.1.call-start = ((), (), s32[]{:S(2)}) async-start(), calls=%async_computation.7 | async-start | bytes 4718592 | tf_op jit(solution)/shard_map/reduce_scatter | solution.py:352
Sparse Core Ops, SparseCore 0:
  10.4 72.8 all-gather.6
  96.0 35.7 all-gather.4
  189.0 46.0 all-gather.8
  396.6 47.8 reduce-scatter.1
where the time goes:
time: 454 us; the launch traced here: 453 us
  waiting for transfers between devices  231 us (51%)
  blocking collectives  74.8 us (16%)
  matrix products  59.2 us (13%)
  Pallas kernels  33.1 us (7%)
  other arithmetic  15.3 us (3%)
  between operations  14.2 us (3%)
  starting transfers between devices  13.3 us (3%)
  local copies, waits for them, and re-layouts  12.3 us (3%)
    all_gather x1, waiting for transfers between devices, on_device(): lax.all_gather(jnp.stack([q_new, k_new, v_new], 1), 'req', axis=0, tiled=...  73.3 us
    all_to_all x1, blocking collectives, on_device(): lax.all_to_all(outgoing.reshape(group_count, units, blocks * most_slots,...  51.9 us
    reduce_scatter x1, waiting for transfers between devices, on_device(): lax.psum_scatter(partial.reshape(group_width, slots_here, local_rows, mod...  48 us
    all_to_all x1, waiting for transfers between devices, on_device(): lax.all_to_all(reply, 'req', split_axis=0, concat_axis=0, tiled=True)  39.6 us
    all_to_all x1, waiting for transfers between devices, on_device(): lax.all_to_all(fresh_out, 'exp', split_axis=0, concat_axis=0, tiled=True)  34.5 us
    pallas_call x1, Pallas kernels, attend(): pl.pallas_call(functools.partial(attend_kernel, sinks, tile_keys, tile_ro...  33.1 us
    dot_general x2, matrix products, on_device(): reply = jnp.dot(active, w_down[span], preferred_element_type=jnp.float32)  27.2 us
    all_gather x1, waiting for transfers between devices, on_device(): lax.all_gather(normed, 'exp', axis=0)  21.5 us
  transfers between devices with their start and end apart: 7, of which 6 were waited for; matrix products, arithmetic and copies ran while one was open for 3% of the time, Pallas kernels for 7%

commit v1 on v0

--- a/solution.py
+++ b/solution.py
@@ -1,4 +1,5 @@
 import functools
+import itertools
 
 import jax
 import jax.numpy as jnp
@@ -216,6 +217,49 @@
     )(length.reshape(1), fresh, cycle_cache, sink_wide, cosine, sine)
 
 
+def from_holders(held, slot_request, requests):
+    slots_here = held.shape[0]
+    group_count = lax.axis_size("req")
+    if slots_here != 2 or group_count > 4:
+        return jnp.take(lax.all_gather(held, "req", axis=0, tiled=True), requests, axis=0)
+    group_index = lax.axis_index("req")
+    slot_of = jnp.argsort(slot_request)
+    flips = jnp.array(list(itertools.product(range(2), repeat=group_count)), jnp.int32)
+    colours = (flips[:, :, None] ^ jnp.arange(2, dtype=jnp.int32)).reshape(-1, 2 * group_count)
+    by_request = colours[:, slot_of].reshape(-1, group_count, 2)
+    fits = jnp.all(by_request[..., 0] != by_request[..., 1], axis=1)
+    pick = jnp.argmax(fits)
+    flip = flips[pick]
+    request_colour = by_request[pick]
+    orders = list(itertools.permutations(range(group_count)))
+    table = jnp.array(orders, jnp.int32)
+    slot_groups = jnp.arange(group_count, dtype=jnp.int32)
+    came = []
+    for colour in range(2):
+        source = slot_request[2 * slot_groups + (flip ^ colour)] // 2
+        number = jnp.argmax(jnp.all(table == source, axis=1)).astype(jnp.int32)
+        mine = request_colour[group_index, 1] == colour
+        block = jnp.where(mine, held[1], held[0])
+
+        def moved(order, payload):
+            return lax.ppermute(payload, "req", [(order[g], g) for g in range(group_count)])
+
+        branches = [functools.partial(moved, order) for order in orders]
+        came.append(lax.switch(number, branches, block))
+    swapped = flip[group_index] == 1
+    return jnp.stack(
+        [jnp.where(swapped, came[1], came[0]), jnp.where(swapped, came[0], came[1])]
+    )
+
+
+def swap_all(parts):
+    count = lax.axis_size("req")
+    return [parts[0]] + [
+        lax.ppermute(parts[k], "req", [(g, g ^ k) for g in range(count)])
+        for k in range(1, count)
+    ]
+
+
 def on_device(
     hidden,
     q_new,
@@ -247,8 +291,7 @@
     members_of_slot = head_count // pairs_here
 
     requests = lax.dynamic_slice_in_dim(slot_request, group_index * slots_here, slots_here)
-    fresh_all = lax.all_gather(jnp.stack([q_new, k_new, v_new], 1), "req", axis=0, tiled=True)
-    fresh_sel = jnp.take(fresh_all, requests, axis=0)
+    fresh_sel = from_holders(jnp.stack([q_new, k_new, v_new], 1), slot_request, requests)
     fresh_out = (
         fresh_sel.reshape(
             slots_here, 3, members_of_slot, pairs_here, local_rows, head_dim
@@ -261,8 +304,13 @@
     length = lax.dynamic_index_in_dim(lengths, slot_here, keepdims=False)
 
     hidden_sel = jnp.take(lax.all_gather(hidden, "req", axis=0, tiled=True), requests, axis=0)
-    route_sel = jnp.take(lax.all_gather(routes, "req", axis=0, tiled=True), requests, axis=0)
-    route_group = lax.all_gather(route_sel, "exp", axis=0)
+    route_group = lax.all_gather(routes, ("req", "exp"), axis=0).reshape(
+        group_count, group_width, slots_here, local_rows, -1
+    )
+    route_group = route_group.transpose(0, 2, 1, 3, 4).reshape(
+        group_count * slots_here, group_width, local_rows, -1
+    )
+    route_group = jnp.take(route_group, requests, axis=0)
 
     context, cycle_out = attend(fresh, cycle_cache, sink_cache, length)
     context_rows = lax.all_to_all(context, "exp", split_axis=0, concat_axis=0, tiled=True)
@@ -277,85 +325,85 @@
     inverse = lax.rsqrt(jnp.mean(residual * residual, axis=-1, keepdims=True) + 1e-06)
     normed = (residual * inverse * norm_gain).astype(jnp.bfloat16)
 
-    blocks = group_width * slots_here
     most_slots = max(2, local_rows // 8)
     sub_here = experts_all * SPLIT // devices_all
     units = max(1, sub_here // SPLIT)
     pieces = max(1, SPLIT // sub_here)
-    owners = jnp.arange(group_count, dtype=jnp.int32) * group_width + member_index
+    partners = group_index ^ jnp.arange(group_count, dtype=jnp.int32)
+    owners = partners * group_width + member_index
     served = (
         owners[:, None] * units + jnp.arange(units, dtype=jnp.int32)[None, :]
     ).reshape(-1) // pieces
     served_count = group_count * units
-    route_blocks = route_group.reshape(blocks, local_rows, -1)
-    named = jnp.any(route_blocks[..., None] == served, axis=2)
+    hidden_units = w_gate.shape[1] // units
     earlier_rows = jnp.arange(local_rows)[:, None] > jnp.arange(local_rows)[None, :]
-    earlier = jnp.einsum(
-        "qp,bpe->bqe",
-        earlier_rows.astype(jnp.bfloat16),
-        named.astype(jnp.bfloat16),
-        preferred_element_type=jnp.float32,
-    ).astype(jnp.int32)
-    chosen = named[..., None] & (
-        earlier[..., None] == jnp.arange(most_slots, dtype=jnp.int32)
-    )
-
-    rows_group = lax.all_gather(normed, "exp", axis=0).reshape(blocks, local_rows, model_width)
-    outgoing = jnp.einsum(
-        "bqer,bqd->ebrd",
-        chosen.astype(jnp.bfloat16),
-        rows_group,
-        preferred_element_type=jnp.float32,
-    ).astype(jnp.bfloat16)
-    landed = lax.all_to_all(
-        outgoing.reshape(group_count, units, blocks * most_slots, model_width),
-        "req",
-        split_axis=0,
-        concat_axis=0,
-        tiled=True,
-    )
-    logits = jnp.einsum("bqd,de->bqe", rows_group, router, preferred_element_type=jnp.float32)
-    routed = jnp.any(
-        route_blocks[..., None] == jnp.arange(experts_all, dtype=jnp.int32), axis=2
-    )
-    logits = jnp.where(routed, logits, -jnp.inf)
-    gates_all = jax.nn.softmax(logits, axis=-1)
-    gates = jnp.take(gates_all, served, axis=2)
-    weights = jnp.where(chosen, gates[..., None], 0.0)
-    weights_high = lax.reduce_precision(weights, 8, 7)
-    weights_low = (weights - weights_high).astype(jnp.bfloat16)
-    weights_high = weights_high.astype(jnp.bfloat16)
-
-    hidden_units = w_gate.shape[1] // units
-    replies = []
-    for unit in range(units):
-        rows = landed[:, unit].reshape(group_count * blocks * most_slots, model_width)
-        span = slice(unit * hidden_units, (unit + 1) * hidden_units)
-        gate_part = jnp.dot(rows, w_gate[:, span], preferred_element_type=jnp.float32)
-        up_part = jnp.dot(rows, w_up[:, span], preferred_element_type=jnp.float32)
-        active = (jax.nn.silu(gate_part) * up_part).astype(jnp.bfloat16)
-        reply = jnp.dot(active, w_down[span], preferred_element_type=jnp.float32)
-        replies.append(
-            reply.astype(jnp.bfloat16).reshape(
-                group_count, 1, blocks * most_slots, model_width
+
+    gathered, landed, kept, moe = [], [], [], []
+    for slot in range(slots_here):
+        rows_group = lax.all_gather(normed[slot], "exp", axis=0)
+        gathered.append(rows_group)
+        named = jnp.any(route_group[slot][..., None] == served, axis=2)
+        earlier = jnp.einsum(
+            "qp,bpe->bqe",
+            earlier_rows.astype(jnp.bfloat16),
+            named.astype(jnp.bfloat16),
+            preferred_element_type=jnp.float32,
+        ).astype(jnp.int32)
+        chosen = named[..., None] & (
+            earlier[..., None] == jnp.arange(most_slots, dtype=jnp.int32)
+        )
+        kept.append(chosen)
+        outgoing = jnp.einsum(
+            "bqer,bqd->ebrd",
+            chosen.astype(jnp.bfloat16),
+            rows_group,
+            preferred_element_type=jnp.float32,
+        ).astype(jnp.bfloat16)
+        landed.append(
+            swap_all(outgoing.reshape(group_count, units, group_width * most_slots, model_width))
+        )
+    for slot in range(slots_here):
+        replies = []
+        for unit in range(units):
+            rows = jnp.concatenate([part[unit] for part in landed[slot]], 0)
+            span = slice(unit * hidden_units, (unit + 1) * hidden_units)
+            gate_part = jnp.dot(rows, w_gate[:, span], preferred_element_type=jnp.float32)
+            up_part = jnp.dot(rows, w_up[:, span], preferred_element_type=jnp.float32)
+            active = (jax.nn.silu(gate_part) * up_part).astype(jnp.bfloat16)
+            reply = jnp.dot(active, w_down[span], preferred_element_type=jnp.float32)
+            replies.append(
+                reply.astype(jnp.bfloat16).reshape(
+                    group_count, group_width * most_slots, model_width
+                )
             )
-        )
-    reply = replies[0] if units == 1 else jnp.concatenate(replies, 1)
-    returned = lax.all_to_all(reply, "req", split_axis=0, concat_axis=0, tiled=True).reshape(
-        served_count, blocks, most_slots, model_width
-    )
-
-    def combined(part):
-        return jnp.einsum("bqer,ebrd->bqd", part, returned, preferred_element_type=jnp.float32)
-
-    partial = (combined(weights_high) + combined(weights_low)).astype(jnp.bfloat16)
-    moe = lax.psum_scatter(
-        partial.reshape(group_width, slots_here, local_rows, model_width),
-        "exp",
-        scatter_dimension=0,
-        tiled=False,
-    )
-    layer_out = (residual + moe.astype(jnp.float32)).astype(jnp.bfloat16)
+        back = swap_all(
+            [jnp.stack([reply[k] for reply in replies]) for k in range(group_count)]
+        )
+        returned = jnp.concatenate(back, 0).reshape(
+            served_count, group_width, most_slots, model_width
+        )
+
+        logits = jnp.einsum(
+            "bqd,de->bqe", gathered[slot], router, preferred_element_type=jnp.float32
+        )
+        routed = jnp.any(
+            route_group[slot][..., None] == jnp.arange(experts_all, dtype=jnp.int32), axis=2
+        )
+        gates_all = jax.nn.softmax(jnp.where(routed, logits, -jnp.inf), axis=-1)
+        gates = jnp.take(gates_all, served, axis=2)
+        weights = jnp.where(kept[slot], gates[..., None], 0.0)
+        weights_high = lax.reduce_precision(weights, 8, 7)
+        weights_low = (weights - weights_high).astype(jnp.bfloat16)
+        weights_high = weights_high.astype(jnp.bfloat16)
+
+        def combined(part):
+            return jnp.einsum(
+                "bqer,ebrd->bqd", part, returned, preferred_element_type=jnp.float32
+            )
+
+        partial = (combined(weights_high) + combined(weights_low)).astype(jnp.bfloat16)
+        moe.append(lax.psum_scatter(partial, "exp", scatter_dimension=0, tiled=False))
+    layer_out = (residual + jnp.stack(moe).astype(jnp.float32)).astype(jnp.bfloat16)
     return (layer_out, cycle_out)
 
 

time: 454 us -> 429 us (0.945)
  waiting for transfers between devices: 231 us -> 145 us
  blocking collectives: 74.8 us -> 41.6 us
  matrix products: 59.2 us -> 89.5 us
  local copies, waits for them, and re-layouts: 12.3 us -> 41.3 us
  starting transfers between devices: 13.3 us -> 30.6 us
  other arithmetic: 15.3 us -> 24.7 us
  between operations: 14.2 us -> 19.1 us
    all_gather x2, waiting for transfers between devices: 94.8 us -> 0.01 us  [on_device(): rows_group = lax.all_gather(normed[slot], 'exp', axis=0)]
    ppermute x0 -> x14, waiting for transfers between devices: none -> 53.8 us  [the longest x2 33.8 us: moved(): lax.ppermute(payload, 'req', [(order[g], g) for g in range(group_count)])]
    all_to_all x1 -> x0, blocking collectives: 51.9 us -> none  [on_device(): lax.all_to_all(outgoing.reshape(group_count, units, blocks * most_slots,...]
    all_to_all x1 -> x0, waiting for transfers between devices: 39.6 us -> none  [on_device(): lax.all_to_all(reply, 'req', split_axis=0, concat_axis=0, tiled=True)]
    ppermute x0 -> x14, starting transfers between devices: none -> 21.7 us  [the longest x12 14.1 us: swap_all(): lax.ppermute(parts[k], 'req', [(g, g ^ k) for g in range(count)])]
    all_gather x2 -> x1, blocking collectives: 22.9 us -> 41.6 us  [on_device(): lax.all_gather(routes, ('req', 'exp'), axis=0)]
    dot_general x2 -> x4, matrix products: 27.2 us -> 44.6 us  [on_device(): reply = jnp.dot(active, w_down[span], preferred_element_type=jnp.float32)]
    dot_general x2 -> x4, matrix products: 10.1 us -> 22.8 us  [on_device(): jnp.dot(rows, w_gate[:, span], preferred_element_type=jnp.float32)]
  transfers between devices with their start and end apart: 7 -> 21, of which waited for: 6 -> 7; matrix products, arithmetic and copies ran while one was open for 3% -> 29% of each run, Pallas kernels for 7% -> 8%
where the time goes in v1:
time: 429 us; the launch traced here: 424 us
  waiting for transfers between devices  145 us (34%)
  matrix products  89.5 us (21%)
  blocking collectives  41.6 us (10%)
  local copies, waits for them, and re-layouts  41.3 us (10%)
  Pallas kernels  32.8 us (8%)
  starting transfers between devices  30.6 us (7%)
  other arithmetic  24.7 us (6%)
  between operations  19.1 us (4%)
    dot_general x4, matrix products, on_device(): reply = jnp.dot(active, w_down[span], preferred_element_type=jnp.float32)  44.6 us
    reduce_scatter x2, waiting for transfers between devices, on_device(): lax.psum_scatter(partial, 'exp', scatter_dimension=0, tiled=False)  42.1 us
    all_gather x1, blocking collectives, on_device(): lax.all_gather(routes, ('req', 'exp'), axis=0)  41.6 us
    all_to_all x1, waiting for transfers between devices, on_device(): lax.all_to_all(fresh_out, 'exp', split_axis=0, concat_axis=0, tiled=True)  34.5 us
    ppermute x2, waiting for transfers between devices, moved(): lax.ppermute(payload, 'req', [(order[g], g) for g in range(group_count)])  33.8 us
    pallas_call x1, Pallas kernels, attend(): pl.pallas_call(functools.partial(attend_kernel, sinks, tile_keys, tile_ro...  32.8 us
    dot_general x4, matrix products, on_device(): jnp.dot(rows, w_gate[:, span], preferred_element_type=jnp.float32)  22.8 us
    ppermute x12, waiting for transfers between devices, swap_all(): lax.ppermute(parts[k], 'req', [(g, g ^ k) for g in range(count)])  20 us
  transfers between devices with their start and end apart: 21, of which 7 were waited for; matrix products, arithmetic and copies ran while one was open for 29% of the time, Pallas kernels for 8%

profile of v1, /device:TPU:0, one launch (start us, length us, event | category | flops | bytes accessed | tf_op | source)
XLA Modules:
  0.0 424.3 jit_solution(14446007568541326117)
XLA Ops:
  7.3 1.6 sort.17
  23.6 1.5 pad_maximum_fusion.1
  25.8 20.7 %conditional.2 = (bf16[3,16,64,128]{3,2,1,0:T(8,128)(2,1)}) conditional(s32[]{:T(128)} %clamp.16, bf16[3,16,64,128]{3,2,1,0:T(8,128)(2,1)S(1)} %get-tuple-element.136, bf16[3,16,64,128]{3,2,1,0:T(8,128)(2,1)S(1)} %get-tuple-element.136, bf16[3,16,64,128]{3,2,1,0:T(8,128)(2,1)S(1)} %get-tuple-element.136, ...), branch_computations={%region_5.6_spmd, %region_6.7_spmd, %region_7.8_spmd, %region_8.9_... | conditional | bytes 3145776 | solution.py:248
  25.9 3.0 collective-permute-start.16
  28.9 17.6 %collective-permute-done.16 = bf16[3,16,64,128]{3,2,1,0:T(8,128)(2,1)} collective-permute-done((bf16[3,16,64,128]{3,2,1,0:T(8,128)(2,1)S(1)}, bf16[3,16,64,128]{3,2,1,0:T(8,128)(2,1)}, u32[]{:S(2)}, u32[]{:S(2)}) %collective-permute-start.16) | collective-permute-done | bytes 786464 | tf_op jit(solution)/shard_map/cond/branch_16_fun/ppermute | solution.py:245
  46.6 20.7 %conditional.3 = (bf16[3,16,64,128]{3,2,1,0:T(8,128)(2,1)}) conditional(s32[]{:T(128)} %clamp.17, bf16[3,16,64,128]{3,2,1,0:T(8,128)(2,1)S(1)} %get-tuple-element.137, bf16[3,16,64,128]{3,2,1,0:T(8,128)(2,1)S(1)} %get-tuple-element.137, bf16[3,16,64,128]{3,2,1,0:T(8,128)(2,1)S(1)} %get-tuple-element.137, ...), branch_computations={%region_31.32_spmd, %region_32.33_spmd, %region_33.34_spmd, %regio... | conditional | bytes 3145776 | solution.py:248
  46.6 4.6 %collective-permute-start.35 = (bf16[3,16,64,128]{3,2,1,0:T(8,128)(2,1)S(1)}, bf16[3,16,64,128]{3,2,1,0:T(8,128)(2,1)}, u32[]{:S(2)}, u32[]{:S(2)}) collective-permute-start(bf16[3,16,64,128]{3,2,1,0:T(8,128)(2,1)S(1)} %param.35), channel_id=1, source_target_pairs={{8,0},{24,8},{16,16},{0,24},{9,1},{25,9},{17,17},{1,25},{10,2},{26... | collective-permute-start | bytes 2359304 | tf_op jit(solution)/shard_map/cond/branch_11_fun/ppermute | solution.py:245
  51.1 16.1 %collective-permute-done.35 = bf16[3,16,64,128]{3,2,1,0:T(8,128)(2,1)} collective-permute-done((bf16[3,16,64,128]{3,2,1,0:T(8,128)(2,1)S(1)}, bf16[3,16,64,128]{3,2,1,0:T(8,128)(2,1)}, u32[]{:S(2)}, u32[]{:S(2)}) %collective-permute-start.35) | collective-permute-done | bytes 786464 | tf_op jit(solution)/shard_map/cond/branch_11_fun/ppermute | solution.py:245
  67.9 1.5 select_bitcast_fusion.1
  70.8 4.9 %all-to-all-start = ((bf16[8,3,4,64,128]{4,3,2,1,0:T(8,128)(2,1)}), bf16[8,3,4,64,128]{4,3,2,1,0:T(8,128)(2,1)S(1)}, u32[]{:S(2)}, u32[]{:S(2)}) async-start(bf16[8,3,4,64,128]{4,3,2,1,0:T(8,128)(2,1)} %bitcast.17), calls=%async_computation | async-start | bytes 3145728 | tf_op jit(solution)/shard_map/all_to_all | solution.py:302
  79.0 34.5 %all-to-all-done.fresh_ref = bf16[8,3,4,64,128]{4,3,2,1,0:T(8,128)(2,1)S(1)} async-done(((bf16[8,3,4,64,128]{4,3,2,1,0:T(8,128)(2,1)}), bf16[8,3,4,64,128]{4,3,2,1,0:T(8,128)(2,1)S(1)}, u32[]{:S(2)}, u32[]{:S(2)}) %all-to-all-start) | async-done | bytes 1572896 | tf_op jit(solution)/shard_map/all_to_all | solution.py:302
  113.6 32.8 %shard_map.176 = (bf16[8,4,64,128]{3,2,1,0:T(8,128)(2,1)}, bf16[4,2,4096,128]{3,2,1,0:T(8,128)(2,1)}) custom-call(s32[1]{0:T(128)} %dynamic_slice.19.length_ref, bf16[8,3,4,64,128]{4,3,2,1,0:T(8,128)(2,1)S(1)} %all-to-all-done.fresh_ref, bf16[4,2,4096,128]{3,2,1,0:T(8,128)(2,1)} %cycle_ref.1, bf16[4,2,128,128]{3,2,1,0:T(8,128)(2,1)S(1)} %pad.4.sink_ref, ...), custom_call_target="tpu_custom_call" | custom-call | flops 4831838208 | bytes 16777216 | tf_op jit(solution)/shard_map/pallas_call | solution.py:182
  146.4 3.5 all-to-all-start.1
  150.3 2.2 gather_fusion
  152.5 12.7 %all-to-all-done.1 = bf16[8,4,64,128]{3,2,1,0:T(8,128)(2,1)S(1)} async-done(((bf16[8,4,64,128]{3,2,1,0:T(8,128)(2,1)}), bf16[8,4,64,128]{3,2,1,0:T(8,128)(2,1)S(1)}, u32[]{:S(2)}, u32[]{:S(2)}) %all-to-all-start.1) | async-done | bytes 524320 | tf_op jit(solution)/shard_map/all_to_all | solution.py:316
  165.2 4.9 %multiply_reduce_fusion = (f32[2,64]{1,0:T(2,128)S(1)}, f32[2,64,2048]{2,1,0:T(8,128)S(1)}) fusion(bf16[16,128,2048,1]{2,1,0,3:T(8,128)(2,1)} %bitcast.238, bf16[2,64,2048]{2,1,0:T(8,128)(2,1)S(1)} %gather_fusion, pred[2]{0:T(512)(128)(4,1)S(1)} %get-tuple-element.119, bf16[2,16,64,128]{3,2,1,0:T(8,128)(2,1)S(1)} %bitcast.240), kind=kOutput, calls=%fused_computation.84 | convolution fusion | flops 1075052416 | bytes 10486274 | tf_op jit(solution)/shard_map/shqd,hde->sqe/dot_general | solution.py:318
  171.9 41.6 %all-gather = s32[64,64,6]{1,2,0:T(8,128)S(1)} all-gather(s32[2,64,6]{1,2,0:T(8,128)S(1)} %copy.110), channel_id=2, replica_groups=mesh['req'=4,'exp'=8] {'req','exp'}, dimensions={0}, use_global_device_ids=true | all-gather | bytes 101376 | tf_op jit(solution)/shard_map/all_gather | solution.py:307
  216.8 2.3 fusion.40
  221.9 3.5 collective-permute-start.50
  225.3 4.0 fusion.157
  232.1 4.2 fusion.158
  238.2 1.6 gather_fusion.5
  239.8 1.6 gather_fusion.6
  245.6 1.5 collective-permute-start.55
  247.9 1.4 collective-permute-start.56
  251.6 1.9 slice_bitcast_fusion.23
  254.2 5.6 %fusion.12 = f32[256,1408]{1,0:T(8,128)} fusion(bf16[2048,2816]{1,0:T(8,128)(2,1)} %param.79, bf16[64,2048]{1,0:T(8,128)(2,1)S(1)} %get-tuple-element.154, bf16[64,2048]{1,0:T(8,128)(2,1)S(1)} %get-tuple-element.152, bf16[64,2048]{1,0:T(8,128)(2,1)S(1)} %get-tuple-element.150, bf16[64,2048]{1,0:T(8,128)(2,1)S(1)} %copy-done.11), kind=kOutput, calls=%fused_computation.19 | convolution fusion | flops 1480589312 | bytes 8257536 | tf_op jit(solution)/shard_map/dot_general | solution.py:370
  259.8 8.4 %fusion.60 = bf16[256,2048]{1,0:T(8,128)(2,1)S(1)} fusion(bf16[2816,2048]{1,0:T(8,128)(2,1)} %param.81, bf16[2048,2816]{1,0:T(8,128)(2,1)} %param.80, f32[256,1408]{1,0:T(8,128)} %fusion.12, bf16[64,2048]{1,0:T(8,128)(2,1)} %copy-done.17, bf16[64,2048]{1,0:T(8,128)(2,1)} %copy-done.15, bf16[64,2048]{1,0:T(8,128)(2,1)S(1)} %get-tuple-element.150, ...), kind=kOutput, calls=%fused_computation.51 | convolution fusion | flops 2959671296 | bytes 15073280 | tf_op jit(solution)/shard_map/dot_general | solution.py:373
  269.1 5.7 %fusion.24 = f32[256,1408]{1,0:T(8,128)} fusion(bf16[2048,2816]{1,0:T(8,128)(2,1)} %param.79, bf16[64,2048]{1,0:T(8,128)(2,1)} %get-tuple-element.155, bf16[64,2048]{1,0:T(8,128)(2,1)S(1)} %get-tuple-element.153, bf16[64,2048]{1,0:T(8,128)(2,1)S(1)} %get-tuple-element.151, bf16[64,2048]{1,0:T(8,128)(2,1)S(1)} %copy-done.10), kind=kOutput, calls=%fused_computation.31 | convolution fusion | flops 1480589312 | bytes 8257536 | tf_op jit(solution)/shard_map/dot_general | solution.py:370
  274.8 18.2 %fusion.54 = bf16[256,2048]{1,0:T(8,128)(2,1)S(1)} fusion(bf16[2816,2048]{1,0:T(8,128)(2,1)} %param.81, bf16[2048,2816]{1,0:T(8,128)(2,1)} %param.80, f32[256,1408]{1,0:T(8,128)} %fusion.24, bf16[64,2048]{1,0:T(8,128)(2,1)} %get-tuple-element.155, bf16[64,2048]{1,0:T(8,128)(2,1)} %copy-done.13, bf16[64,2048]{1,0:T(8,128)(2,1)} %copy-done.12, ...), kind=kOutput, calls=%fused_computation.49 | convolution fusion | flops 2959671296 | bytes 15073280 | tf_op jit(solution)/shard_map/dot_general | solution.py:373
  293.1 2.2 pad_maximum_fusion.8
  295.3 1.6 collective-permute-start.53
  299.1 1.4 collective-permute-start.51
  300.5 1.8 slice_bitcast_fusion.9
  302.3 1.9 slice_bitcast_fusion.8
  304.2 1.9 slice_bitcast_fusion.7
  306.7 5.6 %fusion.10 = f32[256,1408]{1,0:T(8,128)} fusion(bf16[2048,2816]{1,0:T(8,128)(2,1)} %param.79, bf16[64,2048]{1,0:T(8,128)(2,1)S(1)} %get-tuple-element.162, bf16[64,2048]{1,0:T(8,128)(2,1)S(1)} %get-tuple-element.160, bf16[64,2048]{1,0:T(8,128)(2,1)S(1)} %get-tuple-element.158, bf16[64,2048]{1,0:T(8,128)(2,1)S(1)} %copy-done.8), kind=kOutput, calls=%fused_computation.17 | convolution fusion | flops 1480589312 | bytes 8257536 | tf_op jit(solution)/shard_map/dot_general | solution.py:370
  312.4 8.4 %fusion.63 = bf16[256,2048]{1,0:T(8,128)(2,1)S(1)} fusion(bf16[2816,2048]{1,0:T(8,128)(2,1)} %param.81, bf16[2048,2816]{1,0:T(8,128)(2,1)} %param.80, f32[256,1408]{1,0:T(8,128)} %fusion.10, bf16[64,2048]{1,0:T(8,128)(2,1)} %copy-done.18, bf16[64,2048]{1,0:T(8,128)(2,1)} %copy-done.16, bf16[64,2048]{1,0:T(8,128)(2,1)} %copy-done.14, ...), kind=kOutput, calls=%fused_computation.52 | convolution fusion | flops 2959671296 | bytes 15073280 | tf_op jit(solution)/shard_map/dot_general | solution.py:373
  321.7 5.9 %fusion.22 = f32[256,1408]{1,0:T(8,128)} fusion(bf16[2048,2816]{1,0:T(8,128)(2,1)} %param.79, bf16[64,2048]{1,0:T(8,128)(2,1)} %get-tuple-element.163, bf16[64,2048]{1,0:T(8,128)(2,1)} %get-tuple-element.161, bf16[64,2048]{1,0:T(8,128)(2,1)} %get-tuple-element.159, bf16[64,2048]{1,0:T(8,128)(2,1)} %get-tuple-element.127), kind=kOutput, calls=%fused_computation.29 | convolution fusion | flops 1480589312 | bytes 8257536 | tf_op jit(solution)/shard_map/dot_general | solution.py:370
  327.6 9.5 %fusion.57 = bf16[256,2048]{1,0:T(8,128)(2,1)} fusion(bf16[2816,2048]{1,0:T(8,128)(2,1)} %param.81, bf16[2048,2816]{1,0:T(8,128)(2,1)} %param.80, f32[256,1408]{1,0:T(8,128)} %fusion.22, bf16[64,2048]{1,0:T(8,128)(2,1)} %get-tuple-element.163, bf16[64,2048]{1,0:T(8,128)(2,1)} %get-tuple-element.161, bf16[64,2048]{1,0:T(8,128)(2,1)} %get-tuple-element.159, ...), kind=kOutput, calls=%fused_computation.50 | convolution fusion | flops 2959671296 | bytes 15073280 | tf_op jit(solution)/shard_map/dot_general | solution.py:373
  342.2 2.1 fusion.27
  346.6 1.6 collective-permute-start.59
  349.0 1.4 collective-permute-start.58
  350.5 20.0 %collective-permute-done.57 = bf16[2,64,2048]{2,1,0:T(8,128)(2,1)S(1)} collective-permute-done((bf16[2,64,2048]{2,1,0:T(8,128)(2,1)S(1)}, bf16[2,64,2048]{2,1,0:T(8,128)(2,1)S(1)}, u32[]{:S(2)}, u32[]{:S(2)}) %collective-permute-start.57) | collective-permute-done | bytes 524320 | tf_op jit(solution)/shard_map/ppermute | solution.py:258
  371.4 2.1 fusion.26
  373.5 5.3 %reduce-scatter.3.cloned.1.call-done = bf16[1,64,2048]{2,1,0:T(8,128)(2,1)} async-done(((bf16[8,64,2048]{2,1,0:T(8,128)(2,1)}), bf16[1,64,2048]{2,1,0:T(8,128)(2,1)}) %reduce-scatter.3.cloned.1.call-update) | async-done | bytes 262160 | tf_op jit(solution)/shard_map/reduce_scatter | solution.py:405
  378.8 36.8 %reduce-scatter.5.cloned.1.call-done = bf16[1,64,2048]{2,1,0:T(8,128)(2,1)} async-done(((bf16[8,64,2048]{2,1,0:T(8,128)(2,1)}), bf16[1,64,2048]{2,1,0:T(8,128)(2,1)}) %reduce-scatter.5.cloned.1.call-update) | async-done | bytes 262160 | tf_op jit(solution)/shard_map/reduce_scatter | solution.py:405
  415.6 1.9 add_convert_fusion
  (174 shorter events, 50.6 us)
Async XLA Ops:
  7.2 218.2 %copy-start = (bf16[2048,64]{0,1:T(8,128)(2,1)S(1)}, bf16[2048,64]{0,1:T(8,128)(2,1)}, u32[]{:S(2)}) copy-start(bf16[2048,64]{0,1:T(8,128)(2,1)} %param.78) | copy-start | bytes 786436
  25.9 20.7 %collective-permute-start.16 = (bf16[3,16,64,128]{3,2,1,0:T(8,128)(2,1)S(1)}, bf16[3,16,64,128]{3,2,1,0:T(8,128)(2,1)}, u32[]{:S(2)}, u32[]{:S(2)}) collective-permute-start(bf16[3,16,64,128]{3,2,1,0:T(8,128)(2,1)S(1)} %param.16), channel_id=1, source_target_pairs={{16,0},{24,8},{0,16},{8,24},{17,1},{25,9},{1,17},{9,25},{18,2},{26... | collective-permute-start | bytes 2359304 | tf_op jit(solution)/shard_map/cond/branch_16_fun/ppermute | solution.py:245
  46.6 20.7 %collective-permute-start.35 = (bf16[3,16,64,128]{3,2,1,0:T(8,128)(2,1)S(1)}, bf16[3,16,64,128]{3,2,1,0:T(8,128)(2,1)}, u32[]{:S(2)}, u32[]{:S(2)}) collective-permute-start(bf16[3,16,64,128]{3,2,1,0:T(8,128)(2,1)S(1)} %param.35), channel_id=1, source_target_pairs={{8,0},{24,8},{16,16},{0,24},{9,1},{25,9},{17,17},{1,25},{10,2},{26... | collective-permute-start | bytes 2359304 | tf_op jit(solution)/shard_map/cond/branch_11_fun/ppermute | solution.py:245
  70.8 5.7 %copy-start.23 = (s32[8]{0:T(128)S(1)}, s32[8]{0:T(128)}, u32[]{:S(2)}) copy-start(s32[8]{0:T(128)} %param.73) | copy-start | bytes 100
  70.8 6.3 %copy-start.20 = (bf16[4,2,4,128]{3,2,1,0:T(4,128)(2,1)S(1)}, bf16[4,2,4,128]{3,2,1,0:T(4,128)(2,1)}, u32[]{:S(2)}) copy-start(bf16[4,2,4,128]{3,2,1,0:T(4,128)(2,1)} %param.75) | copy-start | bytes 24580
  70.8 42.7 %all-to-all-start = ((bf16[8,3,4,64,128]{4,3,2,1,0:T(8,128)(2,1)}), bf16[8,3,4,64,128]{4,3,2,1,0:T(8,128)(2,1)S(1)}, u32[]{:S(2)}, u32[]{:S(2)}) async-start(bf16[8,3,4,64,128]{4,3,2,1,0:T(8,128)(2,1)} %bitcast.17), calls=%async_computation | async-start | bytes 3145728 | tf_op jit(solution)/shard_map/all_to_all | solution.py:302
  75.7 74.6 %all-gather.5.cloned.1.call-start = ((), (), s32[]{:S(2)}) async-start(), calls=%async_computation.4 | async-start | bytes 2621440 | tf_op jit(solution)/shard_map/all_gather | solution.py:306
  113.6 36.6 %copy-start.2 = (s32[8]{0:T(128)S(1)}, s32[8]{0:T(128)}, u32[]{:S(2)}) copy-start(s32[8]{0:T(128)} %param.72) | copy-start | bytes 100
  146.4 18.8 %all-to-all-start.1 = ((bf16[8,4,64,128]{3,2,1,0:T(8,128)(2,1)}), bf16[8,4,64,128]{3,2,1,0:T(8,128)(2,1)S(1)}, u32[]{:S(2)}, u32[]{:S(2)}) async-start(bf16[8,4,64,128]{3,2,1,0:T(8,128)(2,1)} %get-tuple-element.111), calls=%async_computation.1 | async-start | bytes 1048576 | tf_op jit(solution)/shard_map/all_to_all | solution.py:316
  149.9 66.9 %all-gather.7.cloned.1.call-start = ((), (), s32[]{:S(2)}) async-start(), calls=%async_computation.5 | async-start | bytes 2359296 | tf_op jit(solution)/shard_map/all_gather | solution.py:343
  165.2 4.9 %copy-start.19 = (f32[2048]{0:T(1024)S(1)}, f32[2048]{0:T(1024)}, u32[]{:S(2)}) copy-start(f32[2048]{0:T(1024)} %param.77) | copy-start | bytes 24580
  170.0 1.9 copy-start.21
  171.1 61.0 %all-gather.9.cloned.1.call-start = ((), (), s32[]{:S(2)}) async-start(), calls=%async_computation.7 | async-start | bytes 2359296 | tf_op jit(solution)/shard_map/all_gather | solution.py:343
  171.8 207.0 %reduce-scatter.3.cloned.1.call-start = ((), (), s32[]{:S(2)}) async-start(), calls=%async_computation.6 | async-start | bytes 2359296 | tf_op jit(solution)/shard_map/reduce_scatter | solution.py:405
  220.2 27.8 %collective-permute-start.48 = (bf16[2,64,2048]{2,1,0:T(8,128)(2,1)}, bf16[2,64,2048]{2,1,0:T(8,128)(2,1)}, u32[]{:S(2)}, u32[]{:S(2)}) collective-permute-start(bf16[2,64,2048]{2,1,0:T(8,128)(2,1)} %bitcast.235), channel_id=1, source_target_pairs={{0,8},{8,0},{16,24},{24,16},{1,9},{9,1},{17,25},{25,17},{2,10},{10... | collective-permute-start | bytes 1572872 | tf_op jit(solution)/shard_map/ppermute | solution.py:258
  221.0 29.4 %collective-permute-start.49 = (bf16[2,64,2048]{2,1,0:T(8,128)(2,1)}, bf16[2,64,2048]{2,1,0:T(8,128)(2,1)}, u32[]{:S(2)}, u32[]{:S(2)}) collective-permute-start(bf16[2,64,2048]{2,1,0:T(8,128)(2,1)} %bitcast.234), channel_id=1, source_target_pairs={{0,16},{8,24},{16,0},{24,8},{1,17},{9,25},{17,1},{25,9},{2,18},{10... | collective-permute-start | bytes 1572872 | tf_op jit(solution)/shard_map/ppermute | solution.py:258
  221.9 29.7 %collective-permute-start.50 = (bf16[2,64,2048]{2,1,0:T(8,128)(2,1)}, bf16[2,64,2048]{2,1,0:T(8,128)(2,1)}, u32[]{:S(2)}, u32[]{:S(2)}) collective-permute-start(bf16[2,64,2048]{2,1,0:T(8,128)(2,1)} %bitcast.233), channel_id=1, source_target_pairs={{0,24},{8,16},{16,8},{24,0},{1,25},{9,17},{17,9},{25,1},{2,26},{10... | collective-permute-start | bytes 1572872 | tf_op jit(solution)/shard_map/ppermute | solution.py:258
  232.1 9.3 %copy-start.3 = (bf16[8,64,2048]{2,1,0:T(8,128)(2,1)S(1)}, bf16[8,64,2048]{2,1,0:T(8,128)(2,1)}, u32[]{:S(2)}) copy-start(bf16[8,64,2048]{2,1,0:T(8,128)(2,1)} %all-gather.9.cloned.1.call-done) | copy-start | bytes 6291460
  242.1 1.0 copy-start.22
  244.1 55.0 %collective-permute-start.54 = (bf16[2,64,2048]{2,1,0:T(8,128)(2,1)}, bf16[2,64,2048]{2,1,0:T(8,128)(2,1)}, u32[]{:S(2)}, u32[]{:S(2)}) collective-permute-start(bf16[2,64,2048]{2,1,0:T(8,128)(2,1)} %bitcast.232), channel_id=1, source_target_pairs={{0,8},{8,0},{16,24},{24,16},{1,9},{9,1},{17,25},{25,17},{2,10},{10... | collective-permute-start | bytes 1572872 | tf_op jit(solution)/shard_map/ppermute | solution.py:258
  245.6 56.7 %collective-permute-start.55 = (bf16[2,64,2048]{2,1,0:T(8,128)(2,1)}, bf16[2,64,2048]{2,1,0:T(8,128)(2,1)}, u32[]{:S(2)}, u32[]{:S(2)}) collective-permute-start(bf16[2,64,2048]{2,1,0:T(8,128)(2,1)} %bitcast.231), channel_id=1, source_target_pairs={{0,16},{8,24},{16,0},{24,8},{1,17},{9,25},{17,1},{25,9},{2,18},{10... | collective-permute-start | bytes 1572872 | tf_op jit(solution)/shard_map/ppermute | solution.py:258
  247.1 7.1 %copy-start.11 = (bf16[64,2048]{1,0:T(8,128)(2,1)S(1)}, bf16[64,2048]{1,0:T(8,128)(2,1)}, u32[]{:S(2)}) copy-start(bf16[64,2048]{1,0:T(8,128)(2,1)} %get-tuple-element.121) | copy-start | bytes 786436
  247.9 56.2 %collective-permute-start.56 = (bf16[2,64,2048]{2,1,0:T(8,128)(2,1)}, bf16[2,64,2048]{2,1,0:T(8,128)(2,1)}, u32[]{:S(2)}, u32[]{:S(2)}) collective-permute-start(bf16[2,64,2048]{2,1,0:T(8,128)(2,1)} %bitcast.230), channel_id=1, source_target_pairs={{0,24},{8,16},{16,8},{24,0},{1,25},{9,17},{17,9},{25,1},{2,26},{10... | collective-permute-start | bytes 1572872 | tf_op jit(solution)/shard_map/ppermute | solution.py:258
  250.3 18.7 %copy-start.12 = (bf16[64,2048]{1,0:T(8,128)(2,1)}, bf16[64,2048]{1,0:T(8,128)(2,1)S(1)}, u32[]{:S(2)}) copy-start(bf16[64,2048]{1,0:T(8,128)(2,1)S(1)} %get-tuple-element.151) | copy-start | bytes 786436
  251.5 2.0 copy-start.15
  251.5 17.5 %copy-start.13 = (bf16[64,2048]{1,0:T(8,128)(2,1)}, bf16[64,2048]{1,0:T(8,128)(2,1)S(1)}, u32[]{:S(2)}) copy-start(bf16[64,2048]{1,0:T(8,128)(2,1)S(1)} %get-tuple-element.153) | copy-start | bytes 786436
  253.5 0.7 copy-start.17
  259.8 9.3 %copy-start.10 = (bf16[64,2048]{1,0:T(8,128)(2,1)S(1)}, bf16[64,2048]{1,0:T(8,128)(2,1)}, u32[]{:S(2)}) copy-start(bf16[64,2048]{1,0:T(8,128)(2,1)} %get-tuple-element.122) | copy-start | bytes 786436
  293.0 6.1 %copy-start.4 = (bf16[256,2048]{1,0:T(8,128)(2,1)}, bf16[256,2048]{1,0:T(8,128)(2,1)S(1)}, u32[]{:S(2)}) copy-start(bf16[256,2048]{1,0:T(8,128)(2,1)S(1)} %fusion.54) | copy-start | bytes 3145732
  293.0 3.8 copy-start.7
  295.3 45.1 %collective-permute-start.53 = (bf16[2,64,2048]{2,1,0:T(8,128)(2,1)}, bf16[2,64,2048]{2,1,0:T(8,128)(2,1)}, u32[]{:S(2)}, u32[]{:S(2)}) collective-permute-start(bf16[2,64,2048]{2,1,0:T(8,128)(2,1)} %pad_maximum_fusion.8), channel_id=1, source_target_pairs={{0,24},{8,16},{16,8},{24,0},{1,25},{9,17},{17,9},{25,1},{2,26},{10... | collective-permute-start | bytes 1572872 | tf_op jit(solution)/shard_map/ppermute | solution.py:258
  297.7 41.6 %collective-permute-start.52 = (bf16[2,64,2048]{2,1,0:T(8,128)(2,1)}, bf16[2,64,2048]{2,1,0:T(8,128)(2,1)}, u32[]{:S(2)}, u32[]{:S(2)}) collective-permute-start(bf16[2,64,2048]{2,1,0:T(8,128)(2,1)} %pad_maximum_fusion.7), channel_id=1, source_target_pairs={{0,16},{8,24},{16,0},{24,8},{1,17},{9,25},{17,1},{25,9},{2,18},{10... | collective-permute-start | bytes 1572872 | tf_op jit(solution)/shard_map/ppermute | solution.py:258
  298.2 8.5 %copy-start.8 = (bf16[64,2048]{1,0:T(8,128)(2,1)S(1)}, bf16[64,2048]{1,0:T(8,128)(2,1)}, u32[]{:S(2)}) copy-start(bf16[64,2048]{1,0:T(8,128)(2,1)} %get-tuple-element.126) | copy-start | bytes 786436
  299.1 39.0 %collective-permute-start.51 = (bf16[2,64,2048]{2,1,0:T(8,128)(2,1)}, bf16[2,64,2048]{2,1,0:T(8,128)(2,1)}, u32[]{:S(2)}, u32[]{:S(2)}) collective-permute-start(bf16[2,64,2048]{2,1,0:T(8,128)(2,1)} %pad_maximum_fusion.6), channel_id=1, source_target_pairs={{0,8},{8,0},{16,24},{24,16},{1,9},{9,1},{17,25},{25,17},{2,10},{10... | collective-permute-start | bytes 1572872 | tf_op jit(solution)/shard_map/ppermute | solution.py:258
  302.3 3.8 copy-start.14
  304.2 1.9 copy-start.16
  306.0 0.7 copy-start.18
  306.7 5.6 %copy-start.9 = (bf16[64,2048]{1,0:T(8,128)(2,1)S(1)}, bf16[64,2048]{1,0:T(8,128)(2,1)}, u32[]{:S(2)}) copy-start(bf16[64,2048]{1,0:T(8,128)(2,1)} %get-tuple-element.126) | copy-start | bytes 786436
  344.3 1.2 copy-start.5
  344.3 71.3 %reduce-scatter.5.cloned.1.call-start = ((), (), s32[]{:S(2)}) async-start(), calls=%async_computation.8 | async-start | bytes 2359296 | tf_op jit(solution)/shard_map/reduce_scatter | solution.py:405
  345.5 2.7 copy-start.6
  346.6 23.9 %collective-permute-start.59 = (bf16[2,64,2048]{2,1,0:T(8,128)(2,1)S(1)}, bf16[2,64,2048]{2,1,0:T(8,128)(2,1)S(1)}, u32[]{:S(2)}, u32[]{:S(2)}) collective-permute-start(bf16[2,64,2048]{2,1,0:T(8,128)(2,1)S(1)} %pad_maximum_fusion.11), channel_id=1, source_target_pairs={{0,24},{8,16},{16,8},{24,0},{1,25},{9,17},{17,9},{25,1},{2,26},{10... | collective-permute-start | bytes 1572872 | tf_op jit(solution)/shard_map/ppermute | solution.py:258
  348.3 22.1 %collective-permute-start.57 = (bf16[2,64,2048]{2,1,0:T(8,128)(2,1)S(1)}, bf16[2,64,2048]{2,1,0:T(8,128)(2,1)S(1)}, u32[]{:S(2)}, u32[]{:S(2)}) collective-permute-start(bf16[2,64,2048]{2,1,0:T(8,128)(2,1)S(1)} %pad_maximum_fusion.9), channel_id=1, source_target_pairs={{0,8},{8,0},{16,24},{24,16},{1,9},{9,1},{17,25},{25,17},{2,10},{10... | collective-permute-start | bytes 1572872 | tf_op jit(solution)/shard_map/ppermute | solution.py:258
  349.0 21.5 %collective-permute-start.58 = (bf16[2,64,2048]{2,1,0:T(8,128)(2,1)S(1)}, bf16[2,64,2048]{2,1,0:T(8,128)(2,1)S(1)}, u32[]{:S(2)}, u32[]{:S(2)}) collective-permute-start(bf16[2,64,2048]{2,1,0:T(8,128)(2,1)S(1)} %pad_maximum_fusion.10), channel_id=1, source_target_pairs={{0,16},{8,24},{16,0},{24,8},{1,17},{9,25},{17,1},{25,9},{2,18},{10... | collective-permute-start | bytes 1572872 | tf_op jit(solution)/shard_map/ppermute | solution.py:258
  373.5 44.1 %copy-start.1 = (bf16[2048,64]{0,1:T(8,128)(2,1)S(1)}, bf16[2048,64]{0,1:T(8,128)(2,1)}, u32[]{:S(2)}) copy-start(bf16[2048,64]{0,1:T(8,128)(2,1)} %param.78) | copy-start | bytes 786436
Sparse Core Ops, SparseCore 0:
  78.4 37.6 all-gather.4
  171.2 29.9 all-gather.6
  202.8 28.3 all-gather.8
  344.5 34.3 reduce-scatter.2
  381.0 34.5 reduce-scatter.4
